TPU v7x, 32 devices: a whole 2x2x4 slice. The times are simulated.
32 devices in a mesh: gx: 4 (over y, x), gy: 2 (over core), gz: 4 (over z).
Axes of the slice: x: 2, y: 2, z: 4, core: 2. Of those that a mesh axis runs over, the one named last changes fastest.
Arguments:
- earlier_edge_voltage: float32 [6, 32, 32, 1024], P(None, 'gx', 'gy', 'gz'), may hold values from -6 to 6
- coil_drive_current: float32 [6, 32, 32, 1024], P(None, 'gx', 'gy', 'gz'), may hold values from -18 to 18
- sigma_omega_cellwise: float32 [32, 32, 1024], P('gx', 'gy', 'gz'), may hold values from 0.2 to 3
- subdomain_inverse_full: bfloat16 [4, 2, 4, 16, 512, 512], P('gx', 'gy', 'gz'), may hold values from -0.25 to 0.25
- subdomain_inverse_main: float32 [4, 2, 4, 16, 512], P('gx', 'gy', 'gz'), may hold values from 0.25 to 1.75
- subdomain_layer_counts: int32 [4, 2, 4, 16], P('gx', 'gy', 'gz'), may hold values from 1 to 19, 256 in all within a row
- heat_layer_lookup: int32 [4, 8], P('gz'), may hold values from 1 to 96, 256 in all within a row
- warming_amount: float32 [4, 2, 4, 96, 32, 32], P('gx', 'gy', 'gz'), may hold values from 0 to 2
- heat_spreading_coef: float32 [4, 2, 4, 96, 32, 32], P('gx', 'gy', 'gz'), may hold values from 0.25 to 1
Outputs:
- field_new: float32 [6, 32, 32, 1024], P(None, 'gx', 'gy', 'gz')
- renewed_heat_rise: float32 [4, 2, 4, 96, 32, 32], P('gx', 'gy', 'gz')
- renewed_sigma_omega: float32 [32, 32, 1024], P('gx', 'gy', 'gz')
Inputs may be any that keep to these rules, and one draw needn't show every extreme that they name: `subdomain_layer_counts`: each device's 16 segment lengths sum to 256, and every device has a segment of exactly 19 planes. `heat_layer_lookup`: each row sums to 256, and every row has a slab of exactly 96 planes.
All inputs are finite; a program needn't handle non-finite values.
Results may differ from a plain program's by a relative error of at most 0.013.
Values sent between devices are 32-bit elements; how exact they have to be, the bound alone decides.
A program may use at most 128 MiB of HBM per device.

v0:
```python
import functools

import jax
import jax.numpy as jnp
from jax import lax
from jax.experimental import pallas as pl
from jax.experimental.pallas import tpu as pltpu
from jax.sharding import PartitionSpec as P

SWEEPS = 2
SECTIONS = 4
MESH = pl.DeviceIdType.MESH

mass_shift = 1.0
solver_scale = 0.2
coupling_scale = 0.05
time_step = 2.5
heat_drop = 0.15

CHUNK = 64
PAD = 8


def roll(value, shift, axis):
    size = value.shape[axis]
    shift = shift % size
    return value if shift == 0 else pltpu.roll(value, shift, axis)


def remote(src, dst, ssem, rsem, device):
    return pltpu.make_async_remote_copy(
        src_ref=src,
        dst_ref=dst,
        send_sem=ssem,
        recv_sem=rsem,
        device_id=device,
        device_id_type=MESH,
    )


def when_all(entries, act):
    for there, item in entries:

        @pl.when(there)
        def _():
            act(item)


def start_all(entries):
    when_all(entries, lambda copy: copy.start())


def wait_sent(entries):
    when_all(entries, lambda copy: copy.wait_send())


def wait_got(entries):
    when_all(entries, lambda copy: copy.wait_recv())


def greet(entries, others=()):
    barrier = pltpu.get_barrier_semaphore()

    def signal(device):
        pl.semaphore_signal(barrier, inc=1, device_id=device, device_id_type=MESH)

    for device in others:
        signal(device)
    when_all(entries, signal)
    peers = sum([there.astype(jnp.int32) for there, _ in entries], jnp.int32(len(others)))
    pl.semaphore_wait(barrier, peers)


def residual_kernel(
    dims,
    e_ref,
    cur_ref,
    sig_ref,
    res_out,
    field,
    div,
    send_x,
    send_y,
    send_z,
    recv_x,
    recv_y,
    recv_z,
    dsend_x,
    dsend_y,
    dsend_z,
    drecv_x,
    drecv_y,
    drecv_z,
    face_send_sem,
    face_recv_sem,
    div_send_sem,
    div_recv_sem,
):
    gxc, gyc, gzc, cx, cy, cz, nseg, blk, cap = dims
    lanes = cx * cy
    chunks = cz // CHUNK
    gx, gy, gz = lax.axis_index("gx"), lax.axis_index("gy"), lax.axis_index("gz")
    f32 = jnp.float32

    sides = {
        "x+": (gx < gxc - 1, (gx + 1, gy, gz)),
        "x-": (gx > 0, (gx - 1, gy, gz)),
        "y+": (gy < gyc - 1, (gx, gy + 1, gz)),
        "y-": (gy > 0, (gx, gy - 1, gz)),
        "z+": (gz < gzc - 1, (gx, gy, gz + 1)),
        "z-": (gz > 0, (gx, gy, gz - 1)),
    }

    for ref in (recv_x, recv_y, recv_z, drecv_x, drecv_y, drecv_z, send_z, dsend_z):
        ref[...] = jnp.zeros_like(ref)

    for c in range(6):
        field[c, pl.ds(PAD, cz)] = e_ref[c]

    lane = lax.broadcasted_iota(jnp.int32, (CHUNK, lanes), 1)
    lane_x = lane // cy
    lane_y = lane % cy

    def face_copies():
        names = ["x+", "x-", "y+", "y-", "z+", "z-"]
        pairs = [
            (send_x.at[0], recv_x.at[0]),
            (send_x.at[1], recv_x.at[1]),
            (send_y.at[0], recv_y.at[0]),
            (send_y.at[1], recv_y.at[1]),
            (send_z.at[0], recv_z.at[0]),
            (send_z.at[1], recv_z.at[1]),
        ]
        copies = [
            remote(src, dst, face_send_sem.at[i], face_recv_sem.at[i], sides[n][1])
            for i, (n, (src, dst)) in enumerate(zip(names, pairs))
        ]
        sends = [(sides[n][0], copy) for n, copy in zip(names, copies)]
        back = ["x-", "x+", "y-", "y+", "z-", "z+"]
        gets = [(sides[n][0], copy) for n, copy in zip(back, copies)]
        return sends, gets

    def div_copies():
        names = ["x-", "y-", "z-"]
        pairs = [
            (dsend_x, drecv_x),
            (dsend_y, drecv_y),
            (dsend_z, drecv_z),
        ]
        copies = [
            remote(src, dst, div_send_sem.at[i], div_recv_sem.at[i], sides[n][1])
            for i, (n, (src, dst)) in enumerate(zip(names, pairs))
        ]
        sends = [(sides[n][0], copy) for n, copy in zip(names, copies)]
        gets = [(sides[n][0], copy) for n, copy in zip(["x+", "y+", "z+"], copies)]
        return sends, gets

    def pack_faces():
        @pl.loop(0, chunks)
        def _(i):
            rows = pl.ds(pl.multiple_of(i * CHUNK, CHUNK), CHUNK)
            inner = pl.ds(pl.multiple_of(i * CHUNK + PAD, 8), CHUNK)
            x_hi = jnp.zeros((CHUNK, lanes), f32)
            x_lo, y_hi, y_lo = x_hi, x_hi, x_hi
            for c in range(6):
                v = field[c, inner]
                here = lane_x == c
                x_hi = jnp.where(here, roll(v, cy * (c - cx + 1), 1), x_hi)
                x_lo = jnp.where(here, roll(v, cy * c, 1), x_lo)
                here = lane_y == c
                y_hi = jnp.where(here, roll(v, c - cy + 1, 1), y_hi)
                y_lo = jnp.where(here, roll(v, c, 1), y_lo)
            send_x[0, rows] = x_hi
            send_x[1, rows] = x_lo
            send_y[0, rows] = y_hi
            send_y[1, rows] = y_lo

        for c in range(6):
            send_z[0, pl.ds(c, 1)] = field[c, pl.ds(PAD + cz - 1, 1)]
            send_z[1, pl.ds(c, 1)] = field[c, pl.ds(PAD, 1)]

    pack_faces()
    greet(list(sides.values()))
    sends, gets = face_copies()
    start_all(sends)
    wait_got(gets)
    for c in range(6):
        field[c, pl.ds(PAD - 1, 1)] = recv_z[0, pl.ds(c, 1)]
        field[c, pl.ds(PAD + cz, 1)] = recv_z[1, pl.ds(c, 1)]

    def x_low(v, got, c):
        return jnp.where(lane_x == 0, roll(got, -cy * c, 1), roll(v, cy, 1))

    def x_high(v, got, c):
        return jnp.where(lane_x == cx - 1, roll(got, cy * (cx - 1 - c), 1), roll(v, -cy, 1))

    def y_low(v, got, c):
        return jnp.where(lane_y == 0, roll(got, -c, 1), roll(v, 1, 1))

    def y_high(v, got, c):
        return jnp.where(lane_y == cy - 1, roll(got, cy - 1 - c, 1), roll(v, -1, 1))

    for i in range(chunks):
        z0 = i * CHUNK
        rows = pl.ds(z0, CHUNK)
        for part in range(2):
            cs = [3 * part + k for k in range(3)]
            ex, ey, ez = [field[c, pl.ds(PAD + z0, CHUNK)] for c in cs]
            d = (
                ex
                - x_low(ex, recv_x[0, rows], cs[0])
                + ey
                - y_low(ey, recv_y[0, rows], cs[1])
                + ez
                - field[cs[2], pl.ds(PAD + z0 - 1, CHUNK)]
            )
            div[part, pl.ds(PAD + z0, CHUNK)] = d
            place = 2 * i + part
            dx = roll(d, cy * place, 1)
            dy = roll(d, place, 1)
            if place == 0:
                dsend_x[...] = dx
                dsend_y[...] = dy
            else:
                dsend_x[...] = jnp.where(lane_x == place, dx, dsend_x[...])
                dsend_y[...] = jnp.where(lane_y == place, dy, dsend_y[...])
    for part in range(2):
        dsend_z[pl.ds(part, 1)] = div[part, pl.ds(PAD, 1)]
    dsends, dgets = div_copies()
    start_all(dsends)
    wait_got(dgets)
    rim_z = jnp.where(gz == gzc - 1, 1.0, 0.0)
    for part in range(2):
        top = field[3 * part + 2, pl.ds(PAD + cz - 1, 1)]
        div[part, pl.ds(PAD + cz, 1)] = drecv_z[pl.ds(part, 1)] - rim_z * top

    rim = [
        jnp.where((lane_x == cx - 1) & (gx == gxc - 1), 1.0, 0.0),
        jnp.where((lane_y == cy - 1) & (gy == gyc - 1), 1.0, 0.0),
    ]

    for i in range(chunks):
        z0 = i * CHUNK
        rows = pl.ds(z0, CHUNK)
        sig = sig_ref[rows]
        for part in range(2):
            d = div[part, pl.ds(PAD + z0, CHUNK)]
            place = 2 * i + part
            ahead = [
                x_high(d, drecv_x[...], place),
                y_high(d, drecv_y[...], place),
                div[part, pl.ds(PAD + z0 + 1, CHUNK)],
            ]
            for k in range(3):
                c = 3 * part + k
                e = field[c, pl.ds(PAD + z0, CHUNK)]
                step = ahead[k] - d
                if k < 2:
                    step = step - rim[k] * e
                other = field[(c + 3) % 6, pl.ds(PAD + z0, CHUNK)]
                lap = (
                    x_low(e, recv_x[0, rows], c)
                    + x_high(e, recv_x[1, rows], c)
                    + y_low(e, recv_y[0, rows], c)
                    + y_high(e, recv_y[1, rows], c)
                    + field[c, pl.ds(PAD + z0 - 1, CHUNK)]
                    + field[c, pl.ds(PAD + z0 + 1, CHUNK)]
                    - 6.0 * e
                )
                turn = sig * other
                applied = step - lap + mass_shift * e
                applied = applied - turn if part == 0 else applied + turn
                res_out[c, rows] = cur_ref[c, rows] - applied
    wait_sent(sends)
    wait_sent(dsends)


def solve_kernel(
    dims,
    last,
    ints,
    e_ref,
    res_ref,
    mat_hbm,
    diag_ref,
    group_ref,
    *refs,
):
    gxc, gyc, gzc, cx, cy, cz, nseg, blk, cap = dims
    if last:
        sig_ref, field_out, heat_send, mats, wide, solved, planes, joule, mat_sem = refs
    else:
        field_out, mats, wide, solved, planes, mat_sem = refs
    owners = gxc * gyc
    lanes = cx * cy
    chunks = cz // CHUNK
    at_slot = 2 * nseg
    at_start = at_slot + cz
    f32 = jnp.float32

    copies = [
        pltpu.make_async_copy(mat_hbm.at[s], mats.at[s], mat_sem.at[s]) for s in range(nseg)
    ]
    for copy in copies:
        copy.start()

    lane = lax.broadcasted_iota(jnp.int32, (CHUNK, lanes), 1)
    pick_lane = (lane // cy % 2) * 2 + lane % cy % 2
    block_row = lax.broadcasted_iota(jnp.int32, (blk, lanes), 0)

    wide[pl.ds(0, 24)] = jnp.zeros((24, lanes), f32)
    tail = wide.shape[0] - (cz + 1) * 24
    wide[pl.ds((cz + 1) * 24, tail)] = jnp.zeros((tail, lanes), f32)
    for i in range(chunks):
        z0 = i * CHUNK
        for c in range(6):
            r = res_ref[c, pl.ds(z0, CHUNK)].astype(jnp.bfloat16)
            spread = jnp.dot(r, group_ref[...], preferred_element_type=f32)
            for pq in range(4):
                wide[pl.ds((z0 + 1) * 24 + c * 4 + pq, CHUNK, stride=24), :] = spread[
                    :, pq * lanes : (pq + 1) * lanes
                ]

    for s in range(nseg):
        base = pl.multiple_of(ints[s], 8)
        v = wide[pl.ds(base, blk), :]
        v = jnp.where(block_row < ints[nseg + s], v, 0.0)
        copies[s].wait()
        product = jnp.dot(mats[s], v.astype(jnp.bfloat16), preferred_element_type=f32)
        diag = solver_scale * diag_ref[:, s : s + 1]
        solved[pl.ds(s * blk, blk)] = coupling_scale * product + diag * v

    @pl.loop(0, cz // 8)
    def _(i):
        for j in range(8):
            z = i * 8 + j
            base = pl.multiple_of(ints[at_slot + z], 8)
            planes[pl.ds(pl.multiple_of(z * 24, 8), 24)] = solved[pl.ds(base, 24), :]

    for i in range(chunks):
        z0 = i * CHUNK
        rows = pl.ds(z0, CHUNK)
        total = jnp.zeros((CHUNK, lanes), f32)
        for c in range(6):
            first = z0 * 24 + c * 4
            v = planes[pl.ds(first, CHUNK, stride=24), :]
            for pq in range(1, 4):
                v = jnp.where(pick_lane == pq, planes[pl.ds(first + pq, CHUNK, stride=24), :], v)
            v = e_ref[c, rows] + v
            field_out[c, rows] = v
            total = total + v * v
        if last:
            joule[rows] = 0.5 * sig_ref[rows] * total

    if last:
        joule[pl.ds(cz, cap)] = jnp.zeros((cap, lanes), f32)
        for p in range(owners):
            heat_send[pl.ds(p * cap, cap)] = joule[pl.ds(ints[at_start + p], cap), :]


def heat_kernel(
    dims,
    heat_send,
    temp_ref,
    rate_ref,
    end_ref,
    heat_out,
    back_out,
    heat_recv,
    heat_src,
    state_a,
    state_b,
    end_send,
    end_recv,
    factors,
    back_send,
    back_recv,
    a2a_send_sem,
    a2a_recv_sem,
    end_send_sem,
    end_recv_sem,
):
    gxc, gyc, gzc, cx, cy, cz, nseg, blk, cap = dims
    owners = gxc * gyc
    lanes = cx * cy
    gx, gy, gz = lax.axis_index("gx"), lax.axis_index("gy"), lax.axis_index("gz")
    me = gx * gyc + gy
    f32 = jnp.float32

    last = owners - 1
    up_owner = jnp.where(me == last, 0, me + 1)
    up_gz = jnp.where(me == last, gz + 1, gz)
    down_owner = jnp.where(me == 0, last, me - 1)
    down_gz = jnp.where(me == 0, gz - 1, gz)
    chain = {
        "up": ((me < last) | (gz < gzc - 1), (up_owner // gyc, up_owner % gyc, up_gz)),
        "down": ((me > 0) | (gz > 0), (down_owner // gyc, down_owner % gyc, down_gz)),
    }
    end_recv[...] = jnp.zeros_like(end_recv)

    others = [lax.rem(me + step, owners) for step in range(1, owners)]
    cross_up = (me == last) & (gz < gzc - 1)
    cross_down = (me == 0) & (gz > 0)
    greet(
        [(cross_up, chain["up"][1]), (cross_down, chain["down"][1])],
        [(other // gyc, other % gyc, gz) for other in others],
    )

    def exchange(which, src, dst):
        copies = []
        for step in range(1, owners):
            other = lax.rem(me + step, owners)
            copies.append(
                remote(
                    src.at[pl.ds(pl.multiple_of(other * cap, 8), cap)],
                    dst.at[pl.ds(pl.multiple_of(me * cap, 8), cap)],
                    a2a_send_sem.at[which, step - 1],
                    a2a_recv_sem.at[which, step - 1],
                    (other // gyc, other % gyc, gz),
                )
            )
        for copy in copies:
            copy.start()
        return copies

    def ends(step):
        up = remote(
            end_send.at[step, 0],
            end_recv.at[step, 0],
            end_send_sem.at[step, 0],
            end_recv_sem.at[step, 0],
            chain["up"][1],
        )
        down = remote(
            end_send.at[step, 1],
            end_recv.at[step, 1],
            end_send_sem.at[step, 1],
            end_recv_sem.at[step, 1],
            chain["down"][1],
        )
        sends = [(chain["up"][0], up), (chain["down"][0], down)]
        gets = [(chain["down"][0], up), (chain["up"][0], down)]
        return sends, gets

    def send_ends(step, state):
        total = jnp.zeros((owners, lanes), f32)
        for o in range(0, cap, 8):
            total = total + jnp.sum(end_ref[pl.ds(o, 8)] * state[pl.ds(o + 1, 8)], axis=0)
        end_send[step, 0] = total
        end_send[step, 1] = state[1]
        sends, _ = ends(step)
        start_all(sends)

    mine = pl.ds(pl.multiple_of(me * cap, 8), cap)
    copies = exchange(0, heat_send, heat_recv)

    state_a[pl.ds(1, cap)] = temp_ref[...]
    for state in (state_a, state_b):
        state[0] = jnp.zeros((owners, lanes), f32)
        state[cap + 1] = jnp.zeros((owners, lanes), f32)
    send_ends(0, state_a)

    heat_recv[mine] = heat_send[mine]
    for copy in copies:
        copy.wait()
    for p in range(owners):
        heat_src[pl.ds(p, cap, stride=owners), :] = heat_recv[pl.ds(p * cap, cap)]

    group = 8
    shape = (group, owners, lanes)
    own = lax.broadcasted_iota(jnp.int32, shape, 1)
    at = lax.broadcasted_iota(jnp.int32, shape, 2)
    at_x, at_y = at // cy, at % cy
    own_y = own % gyc

    def beside(v):
        t = roll(v, cy, 2)
        u = jnp.where(own >= gyc, roll(t, gyc, 1), 0.0)
        total = jnp.where(at_x == 0, u, t)
        t = roll(v, -cy, 2)
        u = jnp.where(own < owners - gyc, roll(t, -gyc, 1), 0.0)
        total = total + jnp.where(at_x == cx - 1, u, t)
        u = jnp.where(own_y > 0, roll(roll(v, 1 - cy, 2), 1, 1), 0.0)
        total = total + jnp.where(at_y == 0, u, roll(v, 1, 2))
        u = jnp.where(own_y < gyc - 1, roll(roll(v, cy - 1, 2), -1, 1), 0.0)
        return total + jnp.where(at_y == cy - 1, u, roll(v, -1, 2))

    coef = time_step / (SECTIONS * SECTIONS)
    states = [state_a, state_b]
    for step in range(SECTIONS):
        now, to = states[step % 2], states[1 - step % 2]
        if step > 0:
            send_ends(step, now)
        sends, gets = ends(step)
        wait_got(gets)
        now[0] = end_recv[step, 0]

        @pl.loop(0, cap // group)
        def _(i):
            t0 = i * group
            v = now[pl.ds(t0 + 1, group)]
            above = jnp.broadcast_to(end_recv[step, 1][None], shape)
            end = end_ref[pl.ds(t0, group)]
            up = end * above + (1.0 - end) * now[pl.ds(t0 + 2, group)]
            rates = rate_ref[pl.ds(t0, group)]
            rows = pl.ds(pl.multiple_of(t0 * owners, 8), group * owners)
            heat = heat_src[rows].reshape(shape)
            rate = rates * (beside(v) + now[pl.ds(t0, group)] + up - 6.0 * v) + heat
            if step == 0:
                following = v + coef * rate
            else:
                following = 2.0 * v - to[pl.ds(t0 + 1, group)] + 2.0 * coef * rate
            to[pl.ds(t0 + 1, group)] = following
            if step == SECTIONS - 1:
                heat_out[pl.ds(t0, group)] = following
                factors[rows] = jnp.exp(-heat_drop * following).reshape(group * owners, lanes)

        wait_sent(sends)

    for p in range(owners):
        back_send[pl.ds(p * cap, cap)] = factors[pl.ds(p, cap, stride=owners), :]
    back_recv[mine] = back_send[mine]
    for copy in exchange(1, back_send, back_recv):
        copy.wait()
    back_out[...] = back_recv[...]


def body(
    mesh_shape,
    earlier_edge_voltage,
    coil_drive_current,
    sigma_omega_cellwise,
    subdomain_inverse_full,
    subdomain_inverse_main,
    subdomain_layer_counts,
    heat_layer_lookup,
    warming_amount,
    heat_spreading_coef,
):
    gxc, gyc, gzc = mesh_shape
    owners = gxc * gyc
    cx, cy, cz = sigma_omega_cellwise.shape
    lanes = cx * cy
    nseg, blk = subdomain_inverse_main.shape[3:]
    cap = warming_amount.shape[3]
    f32 = jnp.float32

    seg_len = subdomain_layer_counts[0, 0, 0]
    starts = jnp.cumsum(seg_len) - seg_len
    plane_ids = jnp.arange(cz, dtype=jnp.int32)
    owner_seg = jnp.sum((starts[None, :] <= plane_ids[:, None]).astype(jnp.int32), axis=1) - 1
    own_start = jnp.sum(
        jnp.where(owner_seg[:, None] == jnp.arange(nseg)[None, :], starts[None, :], 0), axis=1
    )
    slots = owner_seg * blk + (plane_ids - own_start + 1) * 24
    slab_len = heat_layer_lookup[0]
    slab_starts = jnp.cumsum(slab_len) - slab_len
    owner_slab = jnp.sum((slab_starts[None, :] <= plane_ids[:, None]).astype(jnp.int32), axis=1) - 1
    slab_start = jnp.sum(
        jnp.where(owner_slab[:, None] == jnp.arange(owners)[None, :], slab_starts[None, :], 0),
        axis=1,
    )
    back = owner_slab * cap + plane_ids - slab_start
    me = lax.axis_index("gx") * gyc + lax.axis_index("gy")
    my_len = jnp.sum(jnp.where(jnp.arange(owners) == me, slab_len, 0))
    ints = jnp.concatenate(
        [starts * 24, (seg_len + 2) * 24, slots, slab_starts]
    ).astype(jnp.int32)

    def planes_first(a):
        return jnp.swapaxes(a.reshape(-1, lanes, cz), 1, 2)

    def onto_tiles(a):
        a = a[0, 0, 0].reshape(cap, gxc, cx, gyc, cy)
        return jnp.transpose(a, (0, 1, 3, 2, 4)).reshape(cap, owners, lanes)

    diag = jnp.pad(subdomain_inverse_main[0, 0, 0].T, ((0, 0), (0, lanes - nseg)))
    source = jnp.arange(lanes)[:, None]
    target = jnp.arange(4 * lanes)[None, :]
    pq, to = target // lanes, target % lanes
    same = ((source // cy // 2) == (to // cy // 2)) & ((source % cy // 2) == (to % cy // 2))
    part = (source // cy % 2) * 2 + source % cy % 2
    group = (same & (part == pq)).astype(jnp.bfloat16)

    vmem = pl.BlockSpec(memory_space=pltpu.VMEM)
    smem = pl.BlockSpec(memory_space=pltpu.SMEM)
    hbm = pl.BlockSpec(memory_space=pl.ANY)
    dims = (gxc, gyc, gzc, cx, cy, cz, nseg, blk, cap)
    whole = jax.ShapeDtypeStruct((6, cz, lanes), f32)
    slabs = jax.ShapeDtypeStruct((owners * cap, lanes), f32)
    dma = pltpu.SemaphoreType.DMA

    def residual(field, sweep):
        return pl.pallas_call(
            functools.partial(residual_kernel, dims),
            out_shape=whole,
            in_specs=[vmem] * 3,
            out_specs=vmem,
            scratch_shapes=[
                pltpu.VMEM((6, cz + 2 * PAD, lanes), f32),
                pltpu.VMEM((2, cz + 2 * PAD, lanes), f32),
                pltpu.VMEM((2, cz, lanes), f32),
                pltpu.VMEM((2, cz, lanes), f32),
                pltpu.VMEM((2, 8, lanes), f32),
                pltpu.VMEM((2, cz, lanes), f32),
                pltpu.VMEM((2, cz, lanes), f32),
                pltpu.VMEM((2, 8, lanes), f32),
                pltpu.VMEM((CHUNK, lanes), f32),
                pltpu.VMEM((CHUNK, lanes), f32),
                pltpu.VMEM((8, lanes), f32),
                pltpu.VMEM((CHUNK, lanes), f32),
                pltpu.VMEM((CHUNK, lanes), f32),
                pltpu.VMEM((8, lanes), f32),
                dma((6,)),
                dma((6,)),
                dma((3,)),
                dma((3,)),
            ],
            compiler_params=pltpu.CompilerParams(
                collective_id=sweep, has_side_effects=True, vmem_limit_bytes=24 * 2**20
            ),
            name="residual",
        )(field, current, sigma_rows)

    def solve(field, res, last):
        extra = [sigma_rows] if last else []
        out = pl.pallas_call(
            functools.partial(solve_kernel, dims, last),
            out_shape=(whole, slabs) if last else (whole,),
            in_specs=[smem, vmem, vmem, hbm, vmem, vmem] + [vmem] * len(extra),
            out_specs=(vmem, vmem) if last else (vmem,),
            scratch_shapes=[
                pltpu.VMEM((nseg, blk, blk), jnp.bfloat16),
                pltpu.VMEM(((cz + blk // 24 + 2) * 24, lanes), f32),
                pltpu.VMEM((nseg * blk, lanes), f32),
                pltpu.VMEM((cz * 24, lanes), f32),
            ]
            + ([pltpu.VMEM((cz + cap, lanes), f32)] if last else [])
            + [dma((nseg,))],
            compiler_params=pltpu.CompilerParams(vmem_limit_bytes=40 * 2**20),
            name="solve",
        )(ints, field, res, solvers, diag, group, *extra)
        return out if last else out[0]

    field = planes_first(earlier_edge_voltage)
    current = planes_first(coil_drive_current)
    sigma_rows = planes_first(sigma_omega_cellwise)[0]
    solvers = subdomain_inverse_full[0, 0, 0]
    for sweep in range(SWEEPS - 1):
        field = solve(field, residual(field, sweep), False)
    field, outgoing = solve(field, residual(field, SWEEPS - 1), True)
    layers = jnp.arange(cap)[:, None, None]
    ends = jnp.broadcast_to((layers + 1 == my_len).astype(f32), (cap, owners, lanes))
    tiles = jax.ShapeDtypeStruct((cap, owners, lanes), f32)
    heat, returned = pl.pallas_call(
        functools.partial(heat_kernel, dims),
        out_shape=(tiles, slabs),
        in_specs=[vmem] * 4,
        out_specs=(vmem, vmem),
        scratch_shapes=[
            pltpu.VMEM((owners * cap, lanes), f32),
            pltpu.VMEM((owners * cap, lanes), f32),
            pltpu.VMEM((cap + 2, owners, lanes), f32),
            pltpu.VMEM((cap + 2, owners, lanes), f32),
            pltpu.VMEM((SECTIONS, 2, owners, lanes), f32),
            pltpu.VMEM((SECTIONS, 2, owners, lanes), f32),
            pltpu.VMEM((owners * cap, lanes), f32),
            pltpu.VMEM((owners * cap, lanes), f32),
            pltpu.VMEM((owners * cap, lanes), f32),
            dma((2, owners - 1)),
            dma((2, owners - 1)),
            dma((SECTIONS, 2)),
            dma((SECTIONS, 2)),
        ],
        compiler_params=pltpu.CompilerParams(
            collective_id=SWEEPS, has_side_effects=True, vmem_limit_bytes=24 * 2**20
        ),
        name="heat",
    )(outgoing, onto_tiles(warming_amount), onto_tiles(heat_spreading_coef), ends)
    heat = jnp.where(layers < my_len, heat, 0.0)
    sigma = sigma_rows * returned[back]
    field_new = jnp.swapaxes(field, 1, 2).reshape(6, cx, cy, cz)
    renewed_sigma = sigma.T.reshape(cx, cy, cz)
    heat = jnp.transpose(heat.reshape(cap, gxc, gyc, cx, cy), (0, 1, 3, 2, 4))
    return (field_new, heat.reshape(1, 1, 1, cap, gxc * cx, gyc * cy), renewed_sigma)


def solution(mesh):
    shape = (mesh.shape["gx"], mesh.shape["gy"], mesh.shape["gz"])
    return jax.shard_map(
        functools.partial(body, shape),
        mesh=mesh,
        in_specs=(
            P(None, "gx", "gy", "gz"),
            P(None, "gx", "gy", "gz"),
            P("gx", "gy", "gz"),
            P("gx", "gy", "gz", None, None, None),
            P("gx", "gy", "gz", None, None),
            P("gx", "gy", "gz", None),
            P("gz", None),
            P("gx", "gy", "gz", None, None, None),
            P("gx", "gy", "gz", None, None, None),
        ),
        out_specs=(
            P(None, "gx", "gy", "gz"),
            P("gx", "gy", "gz", None, None, None),
            P("gx", "gy", "gz"),
        ),
        check_vma=False,
    )
```

profile of v0, /device:TPU:0, one launch (start us, length us, event | category | flops | bytes accessed | tf_op | source)
XLA Modules:
  0.0 99.9 jit_solution(6833717512203959532)
XLA Ops:
  0.6 0.7 copy.47
  1.4 0.1 reduce
  1.5 0.7 broadcast_multiply_fusion.1
  2.2 0.1 convert_reduce_fusion
  2.3 0.1 select_reduce_fusion
  2.4 0.8 reduce-window.13
  3.2 1.3 %fusion.13 = (s32[]{:T(128)}, s32[8]{0:T(128)S(1)}) fusion(s32[1,8]{1,0:T(1,128)} %param.15, s32[]{:T(128)S(6)} %add.196, s32[8,1]{0,1:T(1,128)S(1)} %reduce-window.13), kind=kLoop, calls=%fused_computation.68 | loop fusion | flops 31 | bytes 104 | tf_op jit(solution)/shard_map/reduce_sum | solution.py:565
  4.5 0.1 pad_add_fusion.ints
  4.6 1.0 copy.50
  5.6 1.4 %copy.48 = f32[6,128,256]{1,2,0:T(8,128)S(1)} copy(f32[6,128,256]{2,1,0:T(8,128)} %bitcast.66) | data formatting | bytes 1572864 | tf_op jit(solution)/shard_map/reshape | solution.py:571
  7.0 1.4 %copy.49 = f32[6,128,256]{1,2,0:T(8,128)S(1)} copy(f32[6,128,256]{2,1,0:T(8,128)} %bitcast.67) | data formatting | bytes 1572864 | tf_op jit(solution)/shard_map/reshape | solution.py:571
  8.4 18.3 %residual.2.res_ref = f32[6,256,128]{2,1,0:T(8,128)S(1)} custom-call(f32[6,256,128]{2,1,0:T(8,128)S(1)} %bitcast.56, f32[6,256,128]{2,1,0:T(8,128)S(1)} %bitcast.54, f32[256,128]{1,0:T(8,128)S(1)} %bitcast.58), custom_call_target="tpu_custom_call" | custom-call | tf_op jit(solution)/shard_map/residual/pallas_call | solution.py:594
  26.8 0.1 and_convert_fusion.group_ref
  26.9 0.9 copy.51
  27.8 3.4 %copy-done = bf16[1,1,1,16,512,512]{5,4,3,2,1,0:T(8,128)(2,1)S(1)} copy-done((bf16[1,1,1,16,512,512]{5,4,3,2,1,0:T(8,128)(2,1)S(1)}, bf16[1,1,1,16,512,512]{5,4,3,2,1,0:T(8,128)(2,1)}, u32[]{:S(2)}) %copy-start) | copy-done | bytes 8388632
  31.2 9.9 %solve.2.e_ref = f32[6,256,128]{2,1,0:T(8,128)S(1)} custom-call(s32[296]{0:T(512)S(1)} %pad_add_fusion.ints, f32[6,256,128]{2,1,0:T(8,128)S(1)} %bitcast.57, f32[6,256,128]{2,1,0:T(8,128)S(1)} %residual.2.res_ref, bf16[16,512,512]{2,1,0:T(8,128)(2,1)S(1)} %bitcast.52, f32[512,128]{1,0:T(8,128)S(1)} %pad.4.diag_ref, ...), custom_call_target="tpu_custom_call" | custom-call | tf_op jit(solution)/shard_map/solve/pallas_call | solution.py:627
  41.2 0.0 copy-start.2
  41.2 15.8 %residual.3.res_ref = f32[6,256,128]{2,1,0:T(8,128)S(1)} custom-call(f32[6,256,128]{2,1,0:T(8,128)S(1)} %solve.2.e_ref, f32[6,256,128]{2,1,0:T(8,128)S(1)} %bitcast.55, f32[256,128]{1,0:T(8,128)S(1)} %bitcast.59), custom_call_target="tpu_custom_call" | custom-call | tf_op jit(solution)/shard_map/residual/pallas_call | solution.py:594
  57.0 10.0 %solve.3 = (f32[6,256,128]{2,1,0:T(8,128)S(1)}, f32[768,128]{1,0:T(8,128)S(1)}) custom-call(s32[296]{0:T(512)S(1)} %pad_add_fusion.ints, f32[6,256,128]{2,1,0:T(8,128)S(1)} %solve.2.e_ref, f32[6,256,128]{2,1,0:T(8,128)S(1)} %residual.3.res_ref, bf16[16,512,512]{2,1,0:T(8,128)(2,1)S(1)} %bitcast.53, f32[512,128]{1,0:T(8,128)S(1)} %pad.4.diag_ref, ...), custom_call_target="tpu_custom_call" | custom-call | tf_op jit(solution)/shard_map/solve/pallas_call | solution.py:627
  67.0 0.7 compare_convert_fusion
  67.7 0.2 broadcast_in_dim.37.end_ref
  67.9 0.2 copy.55.temp_ref
  68.2 0.2 copy.56.rate_ref
  68.4 27.4 %heat.1 = (f32[96,8,128]{2,1,0:T(8,128)S(1)}, f32[768,128]{1,0:T(8,128)S(1)}) custom-call(f32[768,128]{1,0:T(8,128)S(1)} %get-tuple-element.8.heat_send, f32[96,8,128]{2,1,0:T(8,128)S(1)} %copy.55.temp_ref, f32[96,8,128]{2,1,0:T(8,128)S(1)} %copy.56.rate_ref, f32[96,8,128]{2,1,0:T(8,128)S(1)} %broadcast_in_dim.37.end_ref), custom_call_target="tpu_custom_call" | custom-call | tf_op jit(solution)/shard_map/heat/pallas_call | solution.py:655
  95.8 0.2 broadcast_select_fusion
  96.0 0.2 copy.57
  96.2 0.9 copy.58
  97.1 0.1 convert_reduce_fusion.1
  97.2 0.1 select_reduce_fusion.1
  97.3 0.7 gather_fusion
  98.0 0.8 copy.59
  98.8 1.1 %copy.52 = f32[6,128,256]{2,1,0:T(8,128)} copy(f32[6,128,256]{1,2,0:T(8,128)S(1)} %bitcast.61) | data formatting | bytes 1572864 | tf_op jit(solution)/shard_map/transpose | solution.py:682
  (23 shorter events, 0.3 us)
Async XLA Ops:
  27.8 3.4 %copy-start = (bf16[1,1,1,16,512,512]{5,4,3,2,1,0:T(8,128)(2,1)S(1)}, bf16[1,1,1,16,512,512]{5,4,3,2,1,0:T(8,128)(2,1)}, u32[]{:S(2)}) copy-start(bf16[1,1,1,16,512,512]{5,4,3,2,1,0:T(8,128)(2,1)} %param.12) | copy-start | bytes 25165828
  31.2 25.8 %copy-start.1 = (bf16[1,1,1,16,512,512]{5,4,3,2,1,0:T(8,128)(2,1)S(1)}, bf16[1,1,1,16,512,512]{5,4,3,2,1,0:T(8,128)(2,1)}, u32[]{:S(2)}) copy-start(bf16[1,1,1,16,512,512]{5,4,3,2,1,0:T(8,128)(2,1)} %param.12) | copy-start | bytes 25165828
  41.2 26.7 %copy-start.2 = (f32[1,1,1,96,32,32]{3,5,4,2,1,0:T(8,128)S(1)}, f32[1,1,1,96,32,32]{3,5,4,2,1,0:T(8,128)}, u32[]{:S(2)}) copy-start(f32[1,1,1,96,32,32]{3,5,4,2,1,0:T(8,128)} %param.16) | copy-start | bytes 1179652
  41.2 26.9 %copy-start.3 = (f32[1,1,1,96,32,32]{3,5,4,2,1,0:T(8,128)S(1)}, f32[1,1,1,96,32,32]{3,5,4,2,1,0:T(8,128)}, u32[]{:S(2)}) copy-start(f32[1,1,1,96,32,32]{3,5,4,2,1,0:T(8,128)} %param.17) | copy-start | bytes 1179652
  57.0 40.0 %copy-start.4 = (s32[1,8]{1,0:T(1,128)S(1)}, s32[1,8]{1,0:T(1,128)}, u32[]{:S(2)}) copy-start(s32[1,8]{1,0:T(1,128)} %param.15) | copy-start | bytes 100
where the time goes:
time: 100 us; the launch traced here: 99.9 us
  Pallas kernels  81.4 us (81%)
  local copies, waits for them, and re-layouts  13.2 us (13%)
  other arithmetic  4.41 us (4%)
    pallas_call x2, Pallas kernels, residual(): pl.pallas_call(functools.partial(residual_kernel, dims), out_shape=whole,...  34.2 us
    pallas_call x1, Pallas kernels, body(): pl.pallas_call(functools.partial(heat_kernel, dims), out_shape=(tiles, sl...  27.4 us
    pallas_call x2, Pallas kernels, solve(): pl.pallas_call(functools.partial(solve_kernel, dims, last), out_shape=(wh...  19.9 us
    unnamed x11, local copies, waits for them, and re-layouts  4.28 us
    reshape x3, local copies, waits for them, and re-layouts, planes_first(): return jnp.swapaxes(a.reshape(-1, lanes, cz), 1, 2)  3.78 us

commit v1 on v0

--- a/solution.py
+++ b/solution.py
@@ -183,6 +183,32 @@
     greet(list(sides.values()))
     sends, gets = face_copies()
     start_all(sends)
+
+    def keep(there, v):
+        return jnp.where(there, v, 0.0)
+
+    for c in range(6):
+        field[c, pl.ds(PAD - 1, 1)] = jnp.zeros((1, lanes), f32)
+        field[c, pl.ds(PAD + cz, 1)] = jnp.zeros((1, lanes), f32)
+    for i in range(chunks):
+        z0 = i * CHUNK
+        rows = pl.ds(z0, CHUNK)
+        sig = sig_ref[rows]
+        for c in range(6):
+            e = field[c, pl.ds(PAD + z0, CHUNK)]
+            turn = sig * field[(c + 3) % 6, pl.ds(PAD + z0, CHUNK)]
+            lap = (
+                keep(lane_x > 0, roll(e, cy, 1))
+                + keep(lane_x < cx - 1, roll(e, -cy, 1))
+                + keep(lane_y > 0, roll(e, 1, 1))
+                + keep(lane_y < cy - 1, roll(e, -1, 1))
+                + field[c, pl.ds(PAD + z0 - 1, CHUNK)]
+                + field[c, pl.ds(PAD + z0 + 1, CHUNK)]
+                - 6.0 * e
+            )
+            rest = cur_ref[c, rows] + lap - mass_shift * e
+            res_out[c, rows] = rest + turn if c < 3 else rest - turn
+
     wait_got(gets)
     for c in range(6):
         field[c, pl.ds(PAD - 1, 1)] = recv_z[0, pl.ds(c, 1)]
@@ -228,6 +254,21 @@
         dsend_z[pl.ds(part, 1)] = div[part, pl.ds(PAD, 1)]
     dsends, dgets = div_copies()
     start_all(dsends)
+    for i in range(chunks):
+        rows = pl.ds(i * CHUNK, CHUNK)
+        for c in range(6):
+            res_out[c, rows] = (
+                res_out[c, rows]
+                + keep(lane_x == 0, roll(recv_x[0, rows], -cy * c, 1))
+                + keep(lane_x == cx - 1, roll(recv_x[1, rows], cy * (cx - 1 - c), 1))
+                + keep(lane_y == 0, roll(recv_y[0, rows], -c, 1))
+                + keep(lane_y == cy - 1, roll(recv_y[1, rows], cy - 1 - c, 1))
+            )
+    for c in range(6):
+        for row, side in ((0, 0), (cz - 1, 1)):
+            at = pl.ds(row, 1)
+            res_out[c, at] = res_out[c, at] + recv_z[side, pl.ds(c, 1)]
+
     wait_got(dgets)
     rim_z = jnp.where(gz == gzc - 1, 1.0, 0.0)
     for part in range(2):
@@ -242,7 +283,6 @@
     for i in range(chunks):
         z0 = i * CHUNK
         rows = pl.ds(z0, CHUNK)
-        sig = sig_ref[rows]
         for part in range(2):
             d = div[part, pl.ds(PAD + z0, CHUNK)]
             place = 2 * i + part
@@ -257,20 +297,7 @@
                 step = ahead[k] - d
                 if k < 2:
                     step = step - rim[k] * e
-                other = field[(c + 3) % 6, pl.ds(PAD + z0, CHUNK)]
-                lap = (
-                    x_low(e, recv_x[0, rows], c)
-                    + x_high(e, recv_x[1, rows], c)
-                    + y_low(e, recv_y[0, rows], c)
-                    + y_high(e, recv_y[1, rows], c)
-                    + field[c, pl.ds(PAD + z0 - 1, CHUNK)]
-                    + field[c, pl.ds(PAD + z0 + 1, CHUNK)]
-                    - 6.0 * e
-                )
-                turn = sig * other
-                applied = step - lap + mass_shift * e
-                applied = applied - turn if part == 0 else applied + turn
-                res_out[c, rows] = cur_ref[c, rows] - applied
+                res_out[c, rows] = res_out[c, rows] - step
     wait_sent(sends)
     wait_sent(dsends)
 
@@ -460,12 +487,6 @@
         state[cap + 1] = jnp.zeros((owners, lanes), f32)
     send_ends(0, state_a)
 
-    heat_recv[mine] = heat_send[mine]
-    for copy in copies:
-        copy.wait()
-    for p in range(owners):
-        heat_src[pl.ds(p, cap, stride=owners), :] = heat_recv[pl.ds(p * cap, cap)]
-
     group = 8
     shape = (group, owners, lanes)
     own = lax.broadcasted_iota(jnp.int32, shape, 1)
@@ -487,29 +508,46 @@
 
     coef = time_step / (SECTIONS * SECTIONS)
     states = [state_a, state_b]
+    heat_recv[mine] = heat_send[mine]
     for step in range(SECTIONS):
         now, to = states[step % 2], states[1 - step % 2]
+        scale = coef if step == 0 else 2.0 * coef
         if step > 0:
             send_ends(step, now)
         sends, gets = ends(step)
-        wait_got(gets)
-        now[0] = end_recv[step, 0]
 
         @pl.loop(0, cap // group)
         def _(i):
             t0 = i * group
+            rows = pl.ds(pl.multiple_of(t0 * owners, 8), group * owners)
             v = now[pl.ds(t0 + 1, group)]
+            up = (1.0 - end_ref[pl.ds(t0, group)]) * now[pl.ds(t0 + 2, group)]
+            rate = rate_ref[pl.ds(t0, group)] * (
+                beside(v) + now[pl.ds(t0, group)] + up - 6.0 * v
+            )
+            if step == 0:
+                to[pl.ds(t0 + 1, group)] = v + scale * rate
+            else:
+                rate = rate + heat_src[rows].reshape(shape)
+                to[pl.ds(t0 + 1, group)] = 2.0 * v - to[pl.ds(t0 + 1, group)] + scale * rate
+
+        if step == 0:
+            for copy in copies:
+                copy.wait()
+            for p in range(owners):
+                heat_src[pl.ds(p, cap, stride=owners), :] = heat_recv[pl.ds(p * cap, cap)]
+        wait_got(gets)
+        to[1] = to[1] + scale * rate_ref[0] * end_recv[step, 0]
+
+        @pl.loop(0, cap // group)
+        def _(i):
+            t0 = i * group
+            rows = pl.ds(pl.multiple_of(t0 * owners, 8), group * owners)
             above = jnp.broadcast_to(end_recv[step, 1][None], shape)
-            end = end_ref[pl.ds(t0, group)]
-            up = end * above + (1.0 - end) * now[pl.ds(t0 + 2, group)]
-            rates = rate_ref[pl.ds(t0, group)]
-            rows = pl.ds(pl.multiple_of(t0 * owners, 8), group * owners)
-            heat = heat_src[rows].reshape(shape)
-            rate = rates * (beside(v) + now[pl.ds(t0, group)] + up - 6.0 * v) + heat
+            extra = rate_ref[pl.ds(t0, group)] * end_ref[pl.ds(t0, group)] * above
             if step == 0:
-                following = v + coef * rate
-            else:
-                following = 2.0 * v - to[pl.ds(t0 + 1, group)] + 2.0 * coef * rate
+                extra = extra + heat_src[rows].reshape(shape)
+            following = to[pl.ds(t0 + 1, group)] + scale * extra
             to[pl.ds(t0 + 1, group)] = following
             if step == SECTIONS - 1:
                 heat_out[pl.ds(t0, group)] = following
@@ -637,7 +675,7 @@
             ]
             + ([pltpu.VMEM((cz + cap, lanes), f32)] if last else [])
             + [dma((nseg,))],
-            compiler_params=pltpu.CompilerParams(vmem_limit_bytes=40 * 2**20),
+            compiler_params=pltpu.CompilerParams(vmem_limit_bytes=60 * 2**20),
             name="solve",
         )(ints, field, res, solvers, diag, group, *extra)
         return out if last else out[0]

time: 100 us -> 97.6 us (0.976)
  Pallas kernels: 81.4 us -> 75.8 us
  local copies, waits for them, and re-layouts: 13.2 us -> 14.7 us
  other arithmetic: 4.41 us -> 5.77 us
    pallas_call x1, Pallas kernels: 27.4 us -> 21.7 us  [body(): pl.pallas_call(functools.partial(heat_kernel, dims), out_shape=(tiles, sl...]
    pallas_call x2, Pallas kernels: 19.9 us -> 23.1 us  [solve(): pl.pallas_call(functools.partial(solve_kernel, dims, last), out_shape=(wh...]
    pallas_call x2, Pallas kernels: 34.2 us -> 31 us  [residual(): pl.pallas_call(functools.partial(residual_kernel, dims), out_shape=whole,...]
    unnamed x11 -> x23, local copies, waits for them, and re-layouts: 4.28 us -> 4.77 us
where the time goes in v1:
time: 97.6 us; the launch traced here: 97.2 us
  Pallas kernels  75.8 us (78%)
  local copies, waits for them, and re-layouts  14.7 us (15%)
  other arithmetic  5.77 us (6%)
    pallas_call x2, Pallas kernels, residual(): pl.pallas_call(functools.partial(residual_kernel, dims), out_shape=whole,...  31 us
    pallas_call x2, Pallas kernels, solve(): pl.pallas_call(functools.partial(solve_kernel, dims, last), out_shape=(wh...  23.1 us
    pallas_call x1, Pallas kernels, body(): pl.pallas_call(functools.partial(heat_kernel, dims), out_shape=(tiles, sl...  21.7 us
    unnamed x23, local copies, waits for them, and re-layouts  4.77 us
    reshape x3, local copies, waits for them, and re-layouts, planes_first(): return jnp.swapaxes(a.reshape(-1, lanes, cz), 1, 2)  4.1 us

profile of v1, /device:TPU:0, one launch (start us, length us, event | category | flops | bytes accessed | tf_op | source)
XLA Modules:
  0.0 97.2 jit_solution(4313963600393898130)
XLA Ops:
  0.6 0.7 copy.47
  1.4 0.1 reduce
  1.5 0.7 broadcast_multiply_fusion.1
  2.3 0.1 select_reduce_fusion
  2.4 0.8 reduce-window.13
  3.2 1.4 %fusion.13 = (s32[]{:T(128)}, s32[8]{0:T(128)S(1)}) fusion(s32[1,8]{1,0:T(1,128)} %param.15, s32[]{:T(128)S(6)} %add.196, s32[8,1]{0,1:T(1,128)S(1)} %reduce-window.13), kind=kLoop, calls=%fused_computation.68 | loop fusion | flops 31 | bytes 104 | tf_op jit(solution)/shard_map/reduce_sum | solution.py:603
  4.6 0.7 pad_add_fusion.ints
  5.2 1.0 %copy.50 = f32[1,128,256]{1,2,0:T(8,128)S(1)} copy(f32[1,128,256]{2,1,0:T(8,128)} %bitcast.72) | data formatting | bytes 262144 | tf_op jit(solution)/shard_map/reshape | solution.py:609
  6.2 1.4 %copy.48 = f32[6,128,256]{1,2,0:T(8,128)S(1)} copy(f32[6,128,256]{2,1,0:T(8,128)} %bitcast.65) | data formatting | bytes 1572864 | tf_op jit(solution)/shard_map/reshape | solution.py:609
  7.7 1.7 %copy.49 = f32[6,128,256]{1,2,0:T(8,128)S(1)} copy(f32[6,128,256]{2,1,0:T(8,128)} %bitcast.66) | data formatting | bytes 1572864 | tf_op jit(solution)/shard_map/reshape | solution.py:609
  9.4 16.8 %residual.2.res_ref = f32[6,256,128]{2,1,0:T(8,128)S(1)} custom-call(f32[6,256,128]{2,1,0:T(8,128)S(1)} %bitcast.54, f32[6,256,128]{2,1,0:T(8,128)S(1)} %bitcast.52, f32[256,128]{1,0:T(8,128)S(1)} %bitcast.56), custom_call_target="tpu_custom_call" | custom-call | tf_op jit(solution)/shard_map/residual/pallas_call | solution.py:632
  26.2 0.9 copy-done.4
  27.1 0.8 and_convert_fusion.group_ref
  27.9 0.9 copy.51
  28.8 0.7 pad.4.diag_ref
  29.5 11.5 %solve.2.e_ref = f32[6,256,128]{2,1,0:T(8,128)} custom-call(s32[296]{0:T(512)} %pad_add_fusion.ints, f32[6,256,128]{2,1,0:T(8,128)} %bitcast.55, f32[6,256,128]{2,1,0:T(8,128)} %copy-done.4, bf16[16,512,512]{2,1,0:T(8,128)(2,1)} %bitcast.59, f32[512,128]{1,0:T(8,128)} %pad.4.diag_ref, bf16[128,512]{1,0:T(8,128)(2,1)} %and_convert_fusion.group_ref), custom_call_target="tpu_custom_call" | custom-call | tf_op jit(solution)/shard_map/solve/pallas_call | solution.py:665
  41.0 1.1 %copy-done.1 = f32[6,256,128]{2,1,0:T(8,128)S(1)} copy-done((f32[6,256,128]{2,1,0:T(8,128)S(1)}, f32[6,256,128]{2,1,0:T(8,128)}, u32[]{:S(2)}) %copy-start.1) | copy-done | bytes 786456
  42.1 14.3 %residual.3.res_ref = f32[6,256,128]{2,1,0:T(8,128)S(1)} custom-call(f32[6,256,128]{2,1,0:T(8,128)S(1)} %copy-done.1, f32[6,256,128]{2,1,0:T(8,128)S(1)} %bitcast.53, f32[256,128]{1,0:T(8,128)S(1)} %bitcast.57), custom_call_target="tpu_custom_call" | custom-call | tf_op jit(solution)/shard_map/residual/pallas_call | solution.py:632
  56.4 0.9 copy-done.5
  57.3 11.6 %solve.3 = (f32[6,256,128]{2,1,0:T(8,128)}, f32[768,128]{1,0:T(8,128)}) custom-call(s32[296]{0:T(512)} %pad_add_fusion.ints, f32[6,256,128]{2,1,0:T(8,128)} %solve.2.e_ref, f32[6,256,128]{2,1,0:T(8,128)} %copy-done.5, bf16[16,512,512]{2,1,0:T(8,128)(2,1)} %bitcast.60, f32[512,128]{1,0:T(8,128)} %pad.4.diag_ref, bf16[128,512]{1,0:T(8,128)(2,1)} %and_convert_fusion.group_ref, ...), custom_call_target="tpu_custom_call" | custom-call | tf_op jit(solution)/shard_map/solve/pallas_call | solution.py:665
  68.9 0.7 compare_convert_fusion
  69.6 0.2 broadcast_in_dim.37.end_ref
  69.8 0.2 copy.55.temp_ref
  70.1 0.2 copy.56.rate_ref
  70.4 1.0 %copy-done.6 = f32[768,128]{1,0:T(8,128)S(1)} copy-done((f32[768,128]{1,0:T(8,128)S(1)}, f32[768,128]{1,0:T(8,128)}, u32[]{:S(2)}) %copy-start.6) | copy-done | bytes 393240
  71.3 21.7 %heat.1 = (f32[96,8,128]{2,1,0:T(8,128)S(1)}, f32[768,128]{1,0:T(8,128)S(1)}) custom-call(f32[768,128]{1,0:T(8,128)S(1)} %copy-done.6, f32[96,8,128]{2,1,0:T(8,128)S(1)} %copy.55.temp_ref, f32[96,8,128]{2,1,0:T(8,128)S(1)} %copy.56.rate_ref, f32[96,8,128]{2,1,0:T(8,128)S(1)} %broadcast_in_dim.37.end_ref), custom_call_target="tpu_custom_call" | custom-call | tf_op jit(solution)/shard_map/heat/pallas_call | solution.py:693
  93.0 0.2 broadcast_select_fusion
  93.2 0.2 copy.57
  93.4 0.9 copy.58
  94.5 0.7 gather_fusion
  95.3 0.8 copy.59
  96.0 1.1 %copy.52 = f32[6,128,256]{2,1,0:T(8,128)} copy(f32[6,128,256]{1,2,0:T(8,128)S(1)} %bitcast.67) | data formatting | bytes 1572864 | tf_op jit(solution)/shard_map/transpose | solution.py:720
  (35 shorter events, 0.5 us)
Async XLA Ops:
  6.2 34.7 %copy-start.2 = (f32[1,128,256]{1,2,0:T(8,128)}, f32[1,128,256]{1,2,0:T(8,128)S(1)}, u32[]{:S(2)}) copy-start(f32[1,128,256]{1,2,0:T(8,128)S(1)} %copy.50) | copy-start | bytes 393220
  7.7 21.8 %copy-start = (f32[6,128,256]{1,2,0:T(8,128)}, f32[6,128,256]{1,2,0:T(8,128)S(1)}, u32[]{:S(2)}) copy-start(f32[6,128,256]{1,2,0:T(8,128)S(1)} %copy.48) | copy-start | bytes 2359300
  26.2 0.9 copy-start.4
  41.0 1.1 %copy-start.1 = (f32[6,256,128]{2,1,0:T(8,128)S(1)}, f32[6,256,128]{2,1,0:T(8,128)}, u32[]{:S(2)}) copy-start(f32[6,256,128]{2,1,0:T(8,128)} %solve.2.e_ref) | copy-start | bytes 2359300
  42.1 27.7 %copy-start.8 = (f32[1,1,1,96,32,32]{3,5,4,2,1,0:T(8,128)S(1)}, f32[1,1,1,96,32,32]{3,5,4,2,1,0:T(8,128)}, u32[]{:S(2)}) copy-start(f32[1,1,1,96,32,32]{3,5,4,2,1,0:T(8,128)} %param.16) | copy-start | bytes 1179652
  42.1 27.9 %copy-start.9 = (f32[1,1,1,96,32,32]{3,5,4,2,1,0:T(8,128)S(1)}, f32[1,1,1,96,32,32]{3,5,4,2,1,0:T(8,128)}, u32[]{:S(2)}) copy-start(f32[1,1,1,96,32,32]{3,5,4,2,1,0:T(8,128)} %param.17) | copy-start | bytes 1179652
  56.4 0.9 copy-start.5
  57.3 37.0 %copy-start.10 = (s32[1,8]{1,0:T(1,128)S(1)}, s32[1,8]{1,0:T(1,128)}, u32[]{:S(2)}) copy-start(s32[1,8]{1,0:T(1,128)} %param.15) | copy-start | bytes 100
  57.3 38.0 %copy-start.3 = (f32[1,128,256]{1,2,0:T(8,128)S(1)}, f32[1,128,256]{1,2,0:T(8,128)}, u32[]{:S(2)}) copy-start(f32[1,128,256]{1,2,0:T(8,128)} %copy-done.2) | copy-start | bytes 393220
  68.9 27.1 %copy-start.7 = (f32[6,256,128]{2,1,0:T(8,128)S(1)}, f32[6,256,128]{2,1,0:T(8,128)}, u32[]{:S(2)}) copy-start(f32[6,256,128]{2,1,0:T(8,128)} %get-tuple-element.7) | copy-start | bytes 2359300
  70.3 1.0 %copy-start.6 = (f32[768,128]{1,0:T(8,128)S(1)}, f32[768,128]{1,0:T(8,128)}, u32[]{:S(2)}) copy-start(f32[768,128]{1,0:T(8,128)} %get-tuple-element.8.heat_send) | copy-start | bytes 1179652
